TPU v7x, 512 devices: a whole 4x4x16 slice. The times are simulated.
512 devices in a mesh: grid: 64 (over z_hi, x, y), mem: 8 (over z_lo, core).
Axes of the slice: x: 4, y: 4, z: 16 (z_hi: 4, z_lo: 4; z = z_hi * 4 + z_lo), core: 2. Of those that a mesh axis runs over, the one named last changes fastest.
Arguments:
- queries: bfloat16 [8, 16384, 1024], P('mem', 'grid'), may hold values from -80 to 80
- keys: bfloat16 [8, 16384, 1024], P('mem', 'grid'), may hold values from -8 to 8
- values: bfloat16 [8, 16384, 1024], P('mem', 'grid'), may hold values from -6 to 6
- truth: bfloat16 [16384, 1024], P('grid'), may hold values from -2 to 2
- widths: int32 [16], replicated, may hold values from 1 to 2, as said below
- node_order: int32 [128], replicated, may hold values from 0 to 127, each once
Outputs:
- query_grads: bfloat16 [8, 16384, 1024], P('mem', 'grid')
- key_grads: bfloat16 [8, 16384, 1024], P('mem', 'grid')
- value_grads: bfloat16 [8, 16384, 1024], P('mem', 'grid')
Inputs may be any that keep to these rules, and one draw needn't show every extreme that they name: `widths`: some head has half-width 2, some head 1.
All inputs are finite; a program needn't handle non-finite values.
Results may differ from a plain program's by a relative error of at most 0.0093.
Values may be sent and summed in bfloat16 or wider, within the bound.
A program may use at most 128 MiB of HBM per device.

v0:
```python
import jax
import jax.numpy as jnp
from jax import lax
from jax.sharding import PartitionSpec as P

HEADS = 16
BLOCK = 128
WMAX = 2


NEG = -1e30
SMOOTH = 0.25


def with_halo(block, sides, width):
    for axis, dim in sides:
        count = lax.axis_size(axis)
        forward = [(i, i + 1) for i in range(count - 1)]
        forward.append((count - 1, 0))
        backward = [(target, source) for source, target in forward]
        low = lax.ppermute(
            lax.slice_in_dim(block, block.shape[dim] - width, None, axis=dim), axis, forward
        )
        high = lax.ppermute(lax.slice_in_dim(block, 0, width, axis=dim), axis, backward)
        block = jnp.concatenate([low, block, high], axis=dim)
    return block


def passed_along(block, axis, distance):
    devices = range(lax.axis_size(axis))
    route = [((i - distance) % len(devices), i) for i in devices]
    return lax.ppermute(block, axis, route)


def window_mask(query_count, key_count, query_shift, key_shift, block_size, widths):
    query_blocks = (
        lax.broadcasted_iota(jnp.int32, (query_count, key_count), 0) // block_size - query_shift
    )
    key_blocks = (
        lax.broadcasted_iota(jnp.int32, (query_count, key_count), 1) // block_size - key_shift
    )
    distance = jnp.abs(query_blocks - key_blocks)
    return distance[None, :, :] <= widths[:, None, None]


def smooth_slope(diff):
    return diff / jnp.sqrt(diff * diff + SMOOTH * SMOOTH)


def crps_grads(own_values, ensemble, target):
    own_f = own_values.astype(jnp.float32)
    total = jnp.zeros_like(own_f)
    members_count = ensemble.shape[0]
    for member in range(members_count):
        total = total + smooth_slope(own_f - ensemble[member].astype(jnp.float32))
    return (smooth_slope(own_f - target.astype(jnp.float32)) - total / (members_count - 1)).astype(
        jnp.bfloat16
    )


def masked_scores(query_part, key_part, allowed, score_scale):
    scores = (
        jnp.einsum("qhd,khd->hqk", query_part, key_part, preferred_element_type=jnp.float32)
        * score_scale
    )
    return jnp.where(allowed, scores, NEG)


def attend_block(query_part, key_part, value_part, allowed, score_scale):
    scores = masked_scores(query_part, key_part, allowed, score_scale)
    highest = jnp.max(scores, axis=2, keepdims=True)
    log_total = highest[:, :, 0] + jnp.log(jnp.sum(jnp.exp(scores - highest), axis=2))
    weights = jnp.exp(scores - log_total[:, :, None]).astype(jnp.bfloat16)
    mixed = jnp.einsum("hqk,khd->qhd", weights, value_part, preferred_element_type=jnp.float32)
    return (mixed, log_total)


def block_grads(
    query_part, grad_part, log_total, inner, key_part, value_part, allowed, score_scale
):
    scores = masked_scores(query_part, key_part, allowed, score_scale)
    weights = jnp.exp(scores - log_total[:, :, None])
    along = jnp.einsum("qhd,khd->hqk", grad_part, value_part, preferred_element_type=jnp.float32)
    dscore = (weights * (along - inner[:, :, None])).astype(jnp.bfloat16)
    query_grad = (
        jnp.einsum("hqk,khd->qhd", dscore, key_part, preferred_element_type=jnp.float32)
        * score_scale
    )
    key_grad = (
        jnp.einsum("hqk,qhd->khd", dscore, query_part, preferred_element_type=jnp.float32)
        * score_scale
    )
    value_grad = jnp.einsum(
        "hqk,qhd->khd", weights.astype(jnp.bfloat16), grad_part, preferred_element_type=jnp.float32
    )
    return (query_grad, key_grad, value_grad)


def on_device(queries, keys, values, truth, widths, node_order):
    query_rows = queries[0]
    key_rows = keys[0]
    value_rows = values[0]
    rows, width = query_rows.shape
    head_dim = width // HEADS
    reach = WMAX * BLOCK
    extended = rows + 2 * reach
    window = BLOCK + 2 * reach
    blocks_here = rows // BLOCK
    score_scale = head_dim ** (-0.5)
    both = with_halo(jnp.stack([key_rows, value_rows]), (("grid", 1),), reach)
    key_ext = both[0]
    value_ext = both[1]

    def split_heads(array):
        return array.reshape(array.shape[0], HEADS, head_dim)

    def rows_at(array, start, count):
        return split_heads(lax.dynamic_slice_in_dim(array, start, count, 0))

    near_allowed = window_mask(BLOCK, window, 0, WMAX, BLOCK, widths)

    def forward_step(block_index, carry):
        mixed_all, totals_all = carry
        start = block_index * BLOCK
        mixed, log_total = attend_block(
            rows_at(query_rows, start, BLOCK),
            rows_at(key_ext, start, window),
            rows_at(value_ext, start, window),
            near_allowed,
            score_scale,
        )
        mixed_all = lax.dynamic_update_slice_in_dim(
            mixed_all, mixed.reshape(BLOCK, width).astype(jnp.bfloat16), start, 0
        )
        totals_all = lax.dynamic_update_slice_in_dim(totals_all, log_total, start, 1)
        return (mixed_all, totals_all)

    outputs, totals = lax.fori_loop(
        0,
        blocks_here,
        forward_step,
        (jnp.zeros((rows, width), jnp.bfloat16), jnp.zeros((HEADS, rows), jnp.float32)),
    )
    target = jnp.take(truth.reshape(blocks_here, BLOCK, width), node_order, axis=1).reshape(
        rows, width
    )
    regrouped = lax.all_to_all(outputs[None], "mem", split_axis=1, concat_axis=0, tiled=True)
    share = regrouped.shape[1]
    target_share = lax.dynamic_slice_in_dim(target, lax.axis_index("mem") * share, share, 0)
    member_grads = crps_grads(regrouped, regrouped, target_share)
    grads = lax.all_to_all(member_grads, "mem", split_axis=0, concat_axis=1, tiled=True)[0]
    inner = jnp.sum(
        (grads.astype(jnp.float32) * outputs.astype(jnp.float32)).reshape(rows, HEADS, head_dim),
        axis=2,
    ).T

    def back_step(block_index, carry):
        query_acc, key_acc, value_acc = carry
        start = block_index * BLOCK
        query_grad, key_grad, value_grad = block_grads(
            rows_at(query_rows, start, BLOCK),
            rows_at(grads, start, BLOCK),
            lax.dynamic_slice_in_dim(totals, start, BLOCK, 1),
            lax.dynamic_slice_in_dim(inner, start, BLOCK, 1),
            rows_at(key_ext, start, window),
            rows_at(value_ext, start, window),
            near_allowed,
            score_scale,
        )
        query_acc = lax.dynamic_update_slice_in_dim(
            query_acc, query_grad.reshape(BLOCK, width).astype(jnp.bfloat16), start, 0
        )
        key_now = lax.dynamic_slice_in_dim(key_acc, start, window, 0) + key_grad.reshape(
            window, width
        )
        value_now = lax.dynamic_slice_in_dim(value_acc, start, window, 0) + value_grad.reshape(
            window, width
        )
        key_acc = lax.dynamic_update_slice_in_dim(key_acc, key_now, start, 0)
        value_acc = lax.dynamic_update_slice_in_dim(value_acc, value_now, start, 0)
        return (query_acc, key_acc, value_acc)

    query_grads, key_ext_grad, value_ext_grad = lax.fori_loop(
        0,
        blocks_here,
        back_step,
        (
            jnp.zeros((rows, width), jnp.bfloat16),
            jnp.zeros((extended, width), jnp.float32),
            jnp.zeros((extended, width), jnp.float32),
        ),
    )
    lower = passed_along(
        jnp.stack([key_ext_grad[:reach], value_ext_grad[:reach]]).astype(jnp.bfloat16), "grid", -1
    ).astype(jnp.float32)
    upper = passed_along(
        jnp.stack([key_ext_grad[extended - reach :], value_ext_grad[extended - reach :]]).astype(
            jnp.bfloat16
        ),
        "grid",
        1,
    ).astype(jnp.float32)
    key_final = (
        key_ext_grad[reach : reach + rows].at[rows - reach :].add(lower[0]).at[:reach].add(upper[0])
    )
    value_final = (
        value_ext_grad[reach : reach + rows]
        .at[rows - reach :]
        .add(lower[1])
        .at[:reach]
        .add(upper[1])
    )
    return (
        query_grads[None],
        key_final.astype(jnp.bfloat16)[None],
        value_final.astype(jnp.bfloat16)[None],
    )


def solution(mesh):
    placed = (
        P("mem", "grid", None),
        P("mem", "grid", None),
        P("mem", "grid", None),
        P("grid", None),
        P(),
        P(),
    )
    return jax.shard_map(
        on_device,
        mesh=mesh,
        in_specs=placed,
        out_specs=(P("mem", "grid", None), P("mem", "grid", None), P("mem", "grid", None)),
        check_vma=False,
    )
```

profile of v0, /device:TPU:1, one launch (start us, length us, event | category | flops | bytes accessed | tf_op | source)
XLA Modules:
  0.0 397.0 jit_solution(14446455039803150928)
XLA Ops:
  0.6 1.3 copy.59
  1.9 1.2 copy.58
  3.3 17.9 %collective-permute-start.1 = (bf16[2,256,1024]{1,2,0:T(8,128)(2,1)S(1)}, bf16[2,256,1024]{1,2,0:T(8,128)(2,1)}, u32[]{:S(2)}, u32[]{:S(2)}) collective-permute-start(bf16[2,256,1024]{1,2,0:T(8,128)(2,1)S(1)} %pad_maximum_fusion.1), channel_id=1, source_target_pairs={{8,0},{16,8},{24,16},{32,24},{40,32},{48,40},{56,48},{64,56},{72,6... | collective-permute-start | bytes 3145736 | tf_op jit(solution)/shard_map/ppermute | solution.py:24
  21.2 1.9 collective-permute-start
  23.6 87.7 %collective-permute-done.1 = bf16[2,256,1024]{1,2,0:T(8,128)(2,1)} collective-permute-done((bf16[2,256,1024]{1,2,0:T(8,128)(2,1)S(1)}, bf16[2,256,1024]{1,2,0:T(8,128)(2,1)}, u32[]{:S(2)}, u32[]{:S(2)}) %collective-permute-start.1) | collective-permute-done | bytes 1048608 | tf_op jit(solution)/shard_map/ppermute | solution.py:24
  111.2 11.4 %collective-permute-done = bf16[2,256,1024]{1,2,0:T(8,128)(2,1)} collective-permute-done((bf16[2,256,1024]{1,2,0:T(8,128)(2,1)S(1)}, bf16[2,256,1024]{1,2,0:T(8,128)(2,1)}, u32[]{:S(2)}, u32[]{:S(2)}) %collective-permute-start) | collective-permute-done | bytes 1048608 | tf_op jit(solution)/shard_map/ppermute | solution.py:21
  122.6 1.6 pad_maximum_fusion
  124.3 1.8 slice_bitcast_fusion
  127.0 15.2 %while.42 = (s32[]{:T(128)}, bf16[256,1024]{0,1:T(8,128)(2,1)}, f32[16,256]{1,0:T(8,128)S(1)}, bf16[768,1024]{0,1:T(8,128)(2,1)}, bf16[256,1024]{0,1:T(8,128)(2,...) while((s32[]{:T(128)}, bf16[256,1024]{0,1:T(8,128)(2,1)}, ...), condition=%wide.region_3.4_spmd.clone, body=%wide.region_0.3_spmd.clone.sunk | while | flops 354023424 | bytes 30409172 | solution.py:138
  127.0 1.9 constant_dynamic-slice_fusion.21
  129.0 1.3 fusion.113
  130.2 1.6 exponential_reduce_fusion.2
  131.9 1.8 fusion.114
  134.6 1.9 constant_dynamic-slice_fusion.21
  136.6 1.3 fusion.113
  137.8 1.6 exponential_reduce_fusion.2
  139.5 1.8 fusion.114
  142.2 2.5 copy.62
  145.3 3.7 reduce.12
  149.0 1.2 reshape.356
  150.1 5.2 %all-to-all-start = ((bf16[8,2,16384]{2,1,0:T(2,128)(2,1)}), bf16[8,2,16384]{2,1,0:T(2,128)(2,1)S(1)}, u32[]{:S(2)}, u32[]{:S(2)}) async-start(bf16[8,2,16384]{2,1,0:T(2,128)(2,1)} %reshape.356), calls=%async_computation | async-start | bytes 1048576 | tf_op jit(solution)/shard_map/all_to_all | solution.py:147
  156.0 1.6 gather_fusion
  158.6 11.3 %all-to-all-done = bf16[8,2,16384]{2,1,0:T(2,128)(2,1)S(1)} async-done(((bf16[8,2,16384]{2,1,0:T(2,128)(2,1)}), bf16[8,2,16384]{2,1,0:T(2,128)(2,1)S(1)}, u32[]{:S(2)}, u32[]{:S(2)}) %all-to-all-start) | async-done | bytes 524320 | tf_op jit(solution)/shard_map/all_to_all | solution.py:147
  172.0 2.7 fusion.44
  174.7 4.9 %all-to-all-start.1 = ((bf16[8,32,1024]{2,1,0:T(8,128)(2,1)}), bf16[8,32,1024]{2,1,0:T(8,128)(2,1)}, u32[]{:S(2)}, u32[]{:S(2)}) async-start(bf16[8,32,1024]{2,1,0:T(8,128)(2,1)} %fusion.44), calls=%async_computation.1 | async-start | bytes 1048576 | tf_op jit(solution)/shard_map/all_to_all | solution.py:151
  179.8 14.4 %all-to-all-done.1 = bf16[8,32,1024]{2,1,0:T(8,128)(2,1)} async-done(((bf16[8,32,1024]{2,1,0:T(8,128)(2,1)}), bf16[8,32,1024]{2,1,0:T(8,128)(2,1)}, u32[]{:S(2)}, u32[]{:S(2)}) %all-to-all-start.1) | async-done | bytes 524320 | tf_op jit(solution)/shard_map/all_to_all | solution.py:151
  194.2 1.2 convert_multiply_fusion
  196.7 2.1 broadcast.248.clone
  198.8 2.1 broadcast.248.clone2
  200.9 87.0 %while.43 = (s32[]{:T(128)}, bf16[256,1024]{1,0:T(8,128)(2,1)}, f32[768,1024]{1,0:T(8,128)}, f32[768,1024]{1,0:T(8,128)}, bf16[768,1024]{0,1:T(8,128)(2,1)}, /*i...) while((s32[]{:T(128)}, bf16[256,1024]{1,0:T(8,128)(2,1)}, ...), condition=%wide.region_6.7_spmd.clone, body=%wide.region_5.6_spmd.clone.sunk | while | flops 856817664 | bytes 161145488 | solution.py:183
  200.9 1.6 constant_dynamic-slice_fusion.23
  203.5 3.2 fusion.125
  207.9 1.4 constant_dynamic-slice_fusion.28
  209.3 3.7 multiply_convert_fusion.2
  213.1 1.1 fusion.126
  215.6 1.9 constant_dynamic-slice_fusion.29
  217.5 2.1 copy.118
  219.6 3.6 fusion.127
  223.5 2.1 copy.119
  225.6 3.5 constant_dynamic-slice_fusion.30
  229.2 3.4 copy.120
  233.2 1.2 copy-done.4
  234.3 1.8 bitcast_add_fusion.5
  236.1 3.4 copy.121
  239.6 4.8 %constant_dynamic-update-slice_fusion.12 = (f32[768,1024]{1,0:T(8,128)}, f32[768,1024]{1,0:T(8,128)}) fusion(f32[768,1024]{1,0:T(8,128)} %get-tuple-element.760, f32[640,1024]{1,0:T(8,128)S(1)} %copy-done.2, s32[]{:T(128)S(6)} %select_n.135, f32[768,1024]{1,0:T(8,128)} %get-tuple-element.759, f32[640,1024]{1,0:T(8,128)} %copy.121), kind=kLoop, calls=%fused_computation.32.clone.1 | loop fusion | bytes 10485764 | tf_op jit(solution)/shard_map/while/body/eval_jaxpr/dynamic_update_slice | solution.py:180
  244.4 1.6 constant_dynamic-slice_fusion.23
  247.0 3.2 fusion.125
  251.4 1.4 constant_dynamic-slice_fusion.28
  252.8 3.7 multiply_convert_fusion.2
  259.1 1.9 constant_dynamic-slice_fusion.29
  261.0 2.1 copy.118
  263.1 3.6 fusion.127
  267.0 2.1 copy.119
  269.1 3.5 constant_dynamic-slice_fusion.30
  272.7 3.4 copy.120
  276.7 1.2 copy-done.4
  277.8 1.8 bitcast_add_fusion.5
  279.7 3.4 copy.121
  283.1 4.8 %constant_dynamic-update-slice_fusion.12 = (f32[768,1024]{1,0:T(8,128)}, f32[768,1024]{1,0:T(8,128)}) fusion(f32[768,1024]{1,0:T(8,128)} %get-tuple-element.760, f32[640,1024]{1,0:T(8,128)S(1)} %copy-done.2, s32[]{:T(128)S(6)} %select_n.135, f32[768,1024]{1,0:T(8,128)} %get-tuple-element.759, f32[640,1024]{1,0:T(8,128)} %copy.121), kind=kLoop, calls=%fused_computation.32.clone.1 | loop fusion | bytes 10485764 | tf_op jit(solution)/shard_map/while/body/eval_jaxpr/dynamic_update_slice | solution.py:180
  287.9 2.3 convert.26
  291.2 1.9 collective-permute-start.3
  293.2 11.5 %collective-permute-start.2 = (bf16[2,256,1024]{2,1,0:T(8,128)(2,1)S(1)}, bf16[2,256,1024]{2,1,0:T(8,128)(2,1)S(1)}, u32[]{:S(2)}, u32[]{:S(2)}) collective-permute-start(bf16[2,256,1024]{2,1,0:T(8,128)(2,1)S(1)} %pad_maximum_fusion.2), channel_id=1, source_target_pairs={{8,0},{16,8},{24,16},{32,24},{40,32},{48,40},{56,48},{64,56},{72,6... | collective-permute-start | bytes 3145736 | tf_op jit(solution)/shard_map/ppermute | solution.py:32
  304.7 89.0 %collective-permute-done.3 = bf16[2,256,1024]{2,1,0:T(8,128)(2,1)S(1)} collective-permute-done((bf16[2,256,1024]{2,1,0:T(8,128)(2,1)S(1)}, bf16[2,256,1024]{2,1,0:T(8,128)(2,1)S(1)}, u32[]{:S(2)}, u32[]{:S(2)}) %collective-permute-start.3) | collective-permute-done | bytes 1048608 | tf_op jit(solution)/shard_map/ppermute | solution.py:32
  394.2 2.8 fusion.74
  (122 shorter events, 19.8 us)
Async XLA Ops:
  0.6 22.5 %copy-start.13 = (bf16[1,256,1024]{2,1,0:T(8,128)(2,1)S(1)}, bf16[1,256,1024]{2,1,0:T(8,128)(2,1)}, u32[]{:S(2)}) copy-start(bf16[1,256,1024]{2,1,0:T(8,128)(2,1)} %param.26) | copy-start | bytes 1572868
  3.3 107.9 %collective-permute-start.1 = (bf16[2,256,1024]{1,2,0:T(8,128)(2,1)S(1)}, bf16[2,256,1024]{1,2,0:T(8,128)(2,1)}, u32[]{:S(2)}, u32[]{:S(2)}) collective-permute-start(bf16[2,256,1024]{1,2,0:T(8,128)(2,1)S(1)} %pad_maximum_fusion.1), channel_id=1, source_target_pairs={{8,0},{16,8},{24,16},{32,24},{40,32},{48,40},{56,48},{64,56},{72,6... | collective-permute-start | bytes 3145736 | tf_op jit(solution)/shard_map/ppermute | solution.py:24
  21.2 101.4 %collective-permute-start = (bf16[2,256,1024]{1,2,0:T(8,128)(2,1)S(1)}, bf16[2,256,1024]{1,2,0:T(8,128)(2,1)}, u32[]{:S(2)}, u32[]{:S(2)}) collective-permute-start(bf16[2,256,1024]{1,2,0:T(8,128)(2,1)S(1)} %pad_maximum_fusion.1), channel_id=1, source_target_pairs={{0,8},{8,16},{16,24},{24,32},{32,40},{40,48},{48,56},{56,64},{64,7... | collective-permute-start | bytes 3145736 | tf_op jit(solution)/shard_map/ppermute | solution.py:21
  124.3 2.7 copy-start.16
  131.9 1.9 copy-start.8
  133.8 0.8 copy-start.9
  139.5 1.9 copy-start.8
  141.4 0.8 copy-start.9
  142.2 13.2 %copy-start.14 = (bf16[256,1024]{1,0:T(8,128)(2,1)S(1)}, bf16[256,1024]{1,0:T(8,128)(2,1)}, u32[]{:S(2)}) copy-start(bf16[256,1024]{1,0:T(8,128)(2,1)} %param.29) | copy-start | bytes 1572868
  142.2 13.7 %copy-start.17 = (s32[128]{0:T(128)S(1)}, s32[128]{0:T(128)}, u32[]{:S(2)}) copy-start(s32[128]{0:T(128)} %param.31) | copy-start | bytes 1540
  150.1 19.7 %all-to-all-start = ((bf16[8,2,16384]{2,1,0:T(2,128)(2,1)}), bf16[8,2,16384]{2,1,0:T(2,128)(2,1)S(1)}, u32[]{:S(2)}, u32[]{:S(2)}) async-start(bf16[8,2,16384]{2,1,0:T(2,128)(2,1)} %reshape.356), calls=%async_computation | async-start | bytes 1048576 | tf_op jit(solution)/shard_map/all_to_all | solution.py:147
  170.4 1.6 copy-start.15
  171.9 7.7 %copy-start.10 = (bf16[256,1024]{0,1:T(8,128)(2,1)S(1)}, bf16[256,1024]{0,1:T(8,128)(2,1)}, u32[]{:S(2)}) copy-start(bf16[256,1024]{0,1:T(8,128)(2,1)} %get-tuple-element.395) | copy-start | bytes 1572868
  174.7 19.5 %all-to-all-start.1 = ((bf16[8,32,1024]{2,1,0:T(8,128)(2,1)}), bf16[8,32,1024]{2,1,0:T(8,128)(2,1)}, u32[]{:S(2)}, u32[]{:S(2)}) async-start(bf16[8,32,1024]{2,1,0:T(8,128)(2,1)} %fusion.44), calls=%async_computation.1 | async-start | bytes 1048576 | tf_op jit(solution)/shard_map/all_to_all | solution.py:151
  200.9 1.6 copy-start.6
  213.0 1.6 copy-start
  213.0 1.7 copy-start.11
  214.8 0.8 copy-start.12
  219.6 3.7 copy-start.3
  229.2 3.4 copy-start.1
  232.6 1.7 copy-start.4
  236.1 3.4 copy-start.2
  239.6 4.8 %copy-start.7 = (bf16[256,1024]{0,1:T(8,128)(2,1)S(1)}, bf16[256,1024]{0,1:T(8,128)(2,1)}, u32[]{:S(2)}) copy-start(bf16[256,1024]{0,1:T(8,128)(2,1)} %copy-done.6) | copy-start | bytes 1572868 | tf_op jit(solution)/shard_map/while
  244.4 1.6 copy-start.6
  256.6 1.6 copy-start
  256.6 1.7 copy-start.11
  258.3 0.8 copy-start.12
  263.1 3.6 copy-start.3
  272.7 3.4 copy-start.1
  276.1 1.7 copy-start.4
  279.7 3.4 copy-start.2
  283.1 4.8 %copy-start.7 = (bf16[256,1024]{0,1:T(8,128)(2,1)S(1)}, bf16[256,1024]{0,1:T(8,128)(2,1)}, u32[]{:S(2)}) copy-start(bf16[256,1024]{0,1:T(8,128)(2,1)} %copy-done.6) | copy-start | bytes 1572868 | tf_op jit(solution)/shard_map/while
  287.9 2.8 copy-start.5
  291.2 102.6 %collective-permute-start.3 = (bf16[2,256,1024]{2,1,0:T(8,128)(2,1)S(1)}, bf16[2,256,1024]{2,1,0:T(8,128)(2,1)S(1)}, u32[]{:S(2)}, u32[]{:S(2)}) collective-permute-start(bf16[2,256,1024]{2,1,0:T(8,128)(2,1)S(1)} %pad_maximum_fusion.3), channel_id=1, source_target_pairs={{504,0},{0,8},{8,16},{16,24},{24,32},{32,40},{40,48},{48,56},{56,6... | collective-permute-start | bytes 3145736 | tf_op jit(solution)/shard_map/ppermute | solution.py:32
  293.2 100.8 %collective-permute-start.2 = (bf16[2,256,1024]{2,1,0:T(8,128)(2,1)S(1)}, bf16[2,256,1024]{2,1,0:T(8,128)(2,1)S(1)}, u32[]{:S(2)}, u32[]{:S(2)}) collective-permute-start(bf16[2,256,1024]{2,1,0:T(8,128)(2,1)S(1)} %pad_maximum_fusion.2), channel_id=1, source_target_pairs={{8,0},{16,8},{24,16},{32,24},{40,32},{48,40},{56,48},{64,56},{72,6... | collective-permute-start | bytes 3145736 | tf_op jit(solution)/shard_map/ppermute | solution.py:32
where the time goes:
time: 398 us; the launch traced here: 397 us
  waiting for transfers between devices  214 us (54%)
  local copies, waits for them, and re-layouts  82.8 us (21%)
  starting transfers between devices  43.4 us (11%)
  matrix products  30.7 us (8%)
  other arithmetic  24.7 us (6%)
    ppermute x2, waiting for transfers between devices, passed_along(): return lax.ppermute(block, axis, route)  89 us
    ppermute x1, waiting for transfers between devices, with_halo(): lax.ppermute(lax.slice_in_dim(block, 0, width, axis=dim), axis, backward)  87.7 us
    ppermute x1, starting transfers between devices, with_halo(): lax.ppermute(lax.slice_in_dim(block, 0, width, axis=dim), axis, backward)  17.9 us
    all_to_all x1, waiting for transfers between devices, on_device(): lax.all_to_all(member_grads, 'mem', split_axis=0, concat_axis=1, tiled=True)  14.4 us
    dynamic_slice x14, local copies, waits for them, and re-layouts, rows_at(): return split_heads(lax.dynamic_slice_in_dim(array, start, count, 0))  14.2 us
    dynamic_slice x4, local copies, waits for them, and re-layouts, back_step(): lax.dynamic_slice_in_dim(key_acc, start, window, 0)  13.9 us
    dynamic_update_slice x4, local copies, waits for them, and re-layouts, back_step(): value_acc = lax.dynamic_update_slice_in_dim(value_acc, value_now, start, 0)  13.8 us
    ppermute x2, starting transfers between devices, passed_along(): return lax.ppermute(block, axis, route)  13.4 us
  transfers between devices with their start and end apart: 6, of which 5 were waited for; matrix products, arithmetic and copies ran while one was open for 1% of the time, Pallas kernels for 0%

commit v1 on v0

v1 whole, which is shorter than its diff:
```python
import functools

import jax
import jax.numpy as jnp
from jax import lax
from jax.experimental import pallas as pl
from jax.experimental.pallas import tpu as pltpu
from jax.sharding import PartitionSpec as P

HEAD = 64
BLOCK = 128
CHUNK = 2 * BLOCK
PLANE = 16
MEM = 8
UNITS = 4
NEG = -1e30
SMOOTH2 = 0.0625
MESH = pl.DeviceIdType.MESH

TN = (((0,), (0,)), ((), ()))
NT = (((1,), (1,)), ((), ()))
NN = (((1,), (0,)), ((), ()))


def dot(a, b, dims):
    return lax.dot_general(a, b, dims, preferred_element_type=jnp.float32)


def slope(diff):
    return diff * lax.rsqrt(diff * diff + SMOOTH2)


def kernel(
    widths, order, q_hbm, k_hbm, v_hbm, t_hbm,
    dq_out, dk_out, dv_out,
    q_in, k_in, v_in, t_in,
    stage, ext, tstage, tgt, weights, out_u, ens, gout, g_u, acc, back_low, back_high,
    dq_src, dkv_src, dq_dst, dkv_dst,
    load_sem, in_send, in_recv, t_send, t_recv, halo_send, halo_recv,
    m1_send, m1_recv, m2_send, m2_recv, back_send, back_recv,
    dq_send, dq_recv, dkv_send, dkv_recv,
):
    grid = lax.axis_index("grid")
    mem = lax.axis_index("mem")
    z_hi = grid // 16
    x = (grid // 4) % 4
    y = grid % 4
    p = grid % 16
    z_lo = mem // 2
    core = mem % 2

    def at_plane(xx, yy):
        return (z_hi * 16 + (xx % 4) * 4 + yy % 4, mem)

    def at_z(d):
        return (((z_hi + d) % 4) * 16 + p, mem)

    truth_from = (1 + z_lo) % 4
    sends_truth = y == truth_from
    loads = [
        pltpu.make_async_copy(src.at[0], dst, load_sem.at[i])
        for i, (src, dst) in enumerate(((q_hbm, q_in), (k_hbm, k_in), (v_hbm, v_in)))
    ]
    for load in loads:
        load.start()
    load_truth = pltpu.make_async_copy(
        t_hbm.at[pl.ds(pl.multiple_of(core * BLOCK, BLOCK), BLOCK)], t_in, load_sem.at[3]
    )
    load_truth.start()

    offsets = [(dx, dy) for dx in (0, 3, 2, 1) for dy in range(4)]
    barrier = pltpu.get_barrier_semaphore()
    for dx, dy in offsets[1:]:
        pl.semaphore_signal(barrier, inc=1, device_id=at_plane(x + dx, y + dy), device_id_type=MESH)
    for o in range(1, MEM):
        pl.semaphore_signal(barrier, inc=1, device_id=(grid, (mem + o) % MEM), device_id_type=MESH)
    for d in (1, 3):
        pl.semaphore_signal(barrier, inc=1, device_id=at_z(d), device_id_type=MESH)

    acc[...] = jnp.zeros_like(acc)
    for load in loads:
        load.wait()

    def to_stage(pair):
        lanes = pl.ds(pl.multiple_of(pair * 128, 128), 128)
        for i, ref in enumerate((q_in, k_in, v_in)):
            block = ref[:, lanes]
            if i == 0:
                block = block * jnp.bfloat16(0.125)
            block = block.T
            stage[pair * 2, pl.ds(i * HEAD, HEAD)] = block[:HEAD]
            stage[pair * 2 + 1, pl.ds(i * HEAD, HEAD)] = block[HEAD:]

    def in_copy(dx, dy):
        target = ((x + dx) % 4) * 4 + (y + dy) % 4
        return pltpu.make_async_remote_copy(
            src_ref=stage.at[target],
            dst_ref=ext.at[1 + p],
            send_sem=in_send.at[dx * 4 + dy],
            recv_sem=in_recv.at[dx * 4 + dy],
            device_id=at_plane(x + dx, y + dy),
            device_id_type=MESH,
        )

    first = True
    for dx in (0, 3, 2, 1):
        row = (x + dx) % 4
        to_stage(row * 2)
        to_stage(row * 2 + 1)
        if first:
            pl.semaphore_wait(barrier, 15 + 7 + 2)
            first = False
        for dy in (1, 3, 2, 0):
            if (dx, dy) != (0, 0):
                in_copy(dx, dy).start()
    ext[1 + p] = stage[p]

    load_truth.wait()

    def t_copy(dx, dy):
        return pltpu.make_async_remote_copy(
            src_ref=tstage.at[((x + dx) % 4) * 4 + (y + dy) % 4],
            dst_ref=tgt.at[dx],
            send_sem=t_send.at[dx * 4 + dy],
            recv_sem=t_recv.at[dx],
            device_id=at_plane(x + dx, y + dy),
            device_id_type=MESH,
        )

    @pl.when(sends_truth)
    def _():
        nodes = lax.broadcasted_iota(jnp.int32, (BLOCK, BLOCK), 0)
        pick = jnp.where(nodes == order[...], 1.0, 0.0).astype(jnp.bfloat16)
        for pair in range(8):
            ordered = dot(t_in[:, pair * 128 : pair * 128 + 128], pick, TN).astype(jnp.bfloat16)
            tstage[pair * 2] = ordered[:HEAD]
            tstage[pair * 2 + 1] = ordered[HEAD:]
        for dx, dy in offsets[1:]:
            t_copy(dx, dy).start()
        tgt[0] = tstage[p]

    far = jnp.where(widths[p] >= 2, 0.0, NEG).astype(jnp.float32)
    second = lax.broadcasted_iota(jnp.int32, (1, CHUNK), 1) >= BLOCK
    rows = lax.broadcasted_iota(jnp.int32, (CHUNK, 1), 0) >= BLOCK
    top_low, bottom_low = jnp.where(second, NEG, far), jnp.where(second, far, 0.0)
    top_high, bottom_high = jnp.where(second, 0.0, far), jnp.where(second, far, NEG)

    def halo_copy(up):
        src, dst = (PLANE, 0) if up else (1, PLANE + 1)
        i = 0 if up else 1
        return pltpu.make_async_remote_copy(
            src_ref=ext.at[src, pl.ds(HEAD, 2 * HEAD)],
            dst_ref=ext.at[dst, pl.ds(HEAD, 2 * HEAD)],
            send_sem=halo_send.at[i],
            recv_sem=halo_recv.at[i],
            device_id=at_z(1 if up else 3),
            device_id_type=MESH,
        )

    def wait_row(k):
        dx = (4 - k) % 4
        for dy in range(4):
            if (dx, dy) != (0, 0):
                in_copy(dx, dy).wait_recv()

        @pl.when((x + k) % 4 == 3)
        def _():
            halo_copy(True).start()

        @pl.when((x + k) % 4 == 0)
        def _():
            halo_copy(False).start()

    def m1_copy(k, o):
        return pltpu.make_async_remote_copy(
            src_ref=out_u.at[k, (mem + o) % MEM],
            dst_ref=ens.at[k, mem],
            send_sem=m1_send.at[k, o],
            recv_sem=m1_recv.at[k, o],
            device_id=(grid, (mem + o) % MEM),
            device_id_type=MESH,
        )

    def m2_copy(k, o):
        return pltpu.make_async_remote_copy(
            src_ref=gout.at[k, (mem + o) % MEM],
            dst_ref=g_u.at[k, mem],
            send_sem=m2_send.at[k, o],
            recv_sem=m2_recv.at[k, o],
            device_id=(grid, (mem + o) % MEM),
            device_id_type=MESH,
        )

    def chunk_of(k, i):
        return (((x + k) % 4) * 4 + 1 + i) % PLANE

    def forward(k):
        @pl.when((x + k) % 4 == 3)
        def _():
            halo_copy(True).wait_recv()
            halo_copy(False).wait_recv()

        def one(i, carry):
            j = chunk_of(k, i)
            q_t = ext[j + 1, pl.ds(0, HEAD)]
            scores = [dot(ext[j + t, pl.ds(HEAD, HEAD)], q_t, TN) for t in range(3)]
            scores[0] = scores[0] + jnp.where(rows, bottom_low, top_low)
            scores[2] = scores[2] + jnp.where(rows, bottom_high, top_high)
            highest = jnp.max(
                jnp.maximum(jnp.maximum(scores[0], scores[1]), scores[2]), axis=0, keepdims=True
            )
            terms = [jnp.exp(s - highest) for s in scores]
            total = jnp.sum(terms[0] + terms[1] + terms[2], axis=0, keepdims=True)
            share = 1.0 / total
            mixed = jnp.zeros((HEAD, CHUNK), jnp.float32)
            for t in range(3):
                low = (terms[t] * share).astype(jnp.bfloat16)
                weights[j, t] = low
                mixed = mixed + dot(ext[j + t, pl.ds(2 * HEAD, HEAD)], low, NN)
            mixed = mixed.astype(jnp.bfloat16)
            out_u[k, 2 * i] = mixed[:, :BLOCK]
            out_u[k, 2 * i + 1] = mixed[:, BLOCK:]
            return carry

        lax.fori_loop(0, 4, one, 0)
        for o in (1, 7, 2, 6, 3, 5, 4):
            m1_copy(k, o).start()
        ens[k, mem] = out_u[k, mem]

    def crps(k):
        dx = (8 - (z_lo // 3) - k) % 4
        if_remote = jnp.logical_not(sends_truth & (dx == 0))

        @pl.when(if_remote)
        def _():
            pltpu.make_async_remote_copy(
                src_ref=tstage.at[0],
                dst_ref=tgt.at[dx],
                send_sem=t_send.at[0],
                recv_sem=t_recv.at[dx],
                device_id=at_plane(x, y + 1),
                device_id_type=MESH,
            ).wait_recv()

        for o in range(1, MEM):
            m1_copy(k, o).wait_recv()
        own = [ens[k, n].astype(jnp.float32) for n in range(MEM)]
        target = tgt[dx].astype(jnp.float32)
        totals = [jnp.zeros((HEAD, BLOCK), jnp.float32) for _ in range(MEM)]
        for a in range(MEM):
            for b in range(a + 1, MEM):
                s = slope(own[a] - own[b])
                totals[a] = totals[a] + s
                totals[b] = totals[b] - s
        for n in range(MEM):
            gout[k, n] = (slope(own[n] - target) - totals[n] * (1.0 / (MEM - 1))).astype(jnp.bfloat16)
        for o in (1, 7, 2, 6, 3, 5, 4):
            m2_copy(k, o).start()
        g_u[k, mem] = gout[k, mem]

    def dq_copy(j):
        return pltpu.make_async_remote_copy(
            src_ref=dq_src.at[j],
            dst_ref=dq_dst.at[p],
            send_sem=dq_send.at[j],
            recv_sem=dq_recv.at[p],
            device_id=(z_hi * 16 + j, mem),
            device_id_type=MESH,
        )

    def dkv_copy(j):
        return pltpu.make_async_remote_copy(
            src_ref=dkv_src.at[j],
            dst_ref=dkv_dst.at[p],
            send_sem=dkv_send.at[j],
            recv_sem=dkv_recv.at[p],
            device_id=(z_hi * 16 + j, mem),
            device_id_type=MESH,
        )

    def send_dkv(j):
        @pl.when(j != p)
        def _():
            dkv_copy(j).start()

        @pl.when(j == p)
        def _():
            dkv_dst[p] = dkv_src[p]

    def back_copy(down):
        i = 0 if down else 1
        return pltpu.make_async_remote_copy(
            src_ref=dkv_src.at[PLANE + i],
            dst_ref=(back_high if down else back_low),
            send_sem=back_send.at[i],
            recv_sem=back_recv.at[i],
            device_id=at_z(3 if down else 1),
            device_id_type=MESH,
        )

    def finish_dkv(j):
        dkv_src[j] = acc[j + 1].astype(jnp.bfloat16)
        send_dkv(j)

    def backward(k):
        for o in range(1, MEM):
            m2_copy(k, o).wait_recv()

        def one(i, carry):
            j = chunk_of(k, i)
            q_t = ext[j + 1, pl.ds(0, HEAD)]
            g_t = jnp.concatenate([g_u[k, 2 * i], g_u[k, 2 * i + 1]], axis=1)
            o_t = jnp.concatenate([out_u[k, 2 * i], out_u[k, 2 * i + 1]], axis=1)
            inner = jnp.sum(g_t.astype(jnp.float32) * o_t.astype(jnp.float32), axis=0, keepdims=True)
            dq = jnp.zeros((HEAD, CHUNK), jnp.float32)
            for t in range(3):
                along = dot(ext[j + t, pl.ds(2 * HEAD, HEAD)], g_t, TN)
                low = weights[j, t]
                ds = (low.astype(jnp.float32) * (along - inner)).astype(jnp.bfloat16)
                dq = dq + dot(ext[j + t, pl.ds(HEAD, HEAD)], ds, NN)
                acc[j + t, pl.ds(0, HEAD)] += dot(q_t, ds, NT)
                acc[j + t, pl.ds(HEAD, HEAD)] += dot(g_t, low, NT)
            dq_src[j] = (dq * 0.125).astype(jnp.bfloat16)

            @pl.when(j != p)
            def _():
                dq_copy(j).start()

            @pl.when(j == p)
            def _():
                dq_dst[p] = dq_src[p]

            return carry

        lax.fori_loop(0, 4, one, 0)

        @pl.when((x + k) % 4 == 3)
        def _():
            dkv_src[PLANE] = acc[0].astype(jnp.bfloat16)
            back_copy(True).start()
            dkv_src[PLANE + 1] = acc[PLANE + 1].astype(jnp.bfloat16)
            back_copy(False).start()

        def done(i, carry):
            j = (((x + k) % 4) * 4 + i) % PLANE

            @pl.when((j != 0) & (j != PLANE - 1))
            def _():
                finish_dkv(j)

            return carry

        if k == 0:
            lax.fori_loop(2, 4, done, 0)
        elif k < UNITS - 1:
            lax.fori_loop(0, 4, done, 0)
        else:
            lax.fori_loop(0, 6, done, 0)

    wait_row(0)
    wait_row(1)
    forward(0)
    wait_row(2)
    forward(1)
    crps(0)
    wait_row(3)
    forward(2)
    crps(1)
    forward(3)
    backward(0)
    crps(2)
    backward(1)
    crps(3)
    backward(2)
    backward(3)

    back_copy(True).wait_recv()
    acc[PLANE] += back_high[...].astype(jnp.float32)
    finish_dkv(PLANE - 1)
    back_copy(False).wait_recv()
    acc[1] += back_low[...].astype(jnp.float32)
    finish_dkv(0)

    def arrived(n, recv):
        src = (p + n) % PLANE
        if recv is dq_recv:
            ref = dq_dst
        else:
            ref = dkv_dst
        pltpu.make_async_remote_copy(
            src_ref=ref.at[src], dst_ref=ref.at[src], send_sem=dq_send.at[0], recv_sem=recv.at[src],
            device_id=(z_hi * 16 + src, mem), device_id_type=MESH,
        ).wait_recv()

    def all_arrived(recv):
        def one(n, carry):
            arrived(n, recv)
            return carry

        lax.fori_loop(1, PLANE, one, 0)

    all_arrived(dq_recv)
    for pair in range(8):
        block = jnp.concatenate([dq_dst[2 * pair], dq_dst[2 * pair + 1]], axis=0)
        dq_out[0, :, pair * 128 : pair * 128 + 128] = block.T
    all_arrived(dkv_recv)
    for pair in range(8):
        for i, ref in enumerate((dk_out, dv_out)):
            block = jnp.concatenate(
                [dkv_dst[2 * pair, pl.ds(i * HEAD, HEAD)], dkv_dst[2 * pair + 1, pl.ds(i * HEAD, HEAD)]],
                axis=0,
            )
            ref[0, :, pair * 128 : pair * 128 + 128] = block.T

    for dx, dy in offsets[1:]:
        in_copy(dx, dy).wait_send()
    for up in (True, False):
        halo_copy(up).wait_send()
        back_copy(up).wait_send()
    for k in range(UNITS):
        for o in range(1, MEM):
            m1_copy(k, o).wait_send()
            m2_copy(k, o).wait_send()

    @pl.when(sends_truth)
    def _():
        for dx, dy in offsets[1:]:
            t_copy(dx, dy).wait_send()

    def sent(n, carry):
        j = (p + n) % PLANE
        dq_copy(j).wait_send()
        dkv_copy(j).wait_send()
        return carry

    lax.fori_loop(1, PLANE, sent, 0)


def on_device(queries, keys, values, truth, widths, node_order):
    bf16 = jnp.bfloat16
    shape = queries.shape
    dma = pltpu.SemaphoreType.DMA
    vmem = pltpu.VMEM
    return pl.pallas_call(
        kernel,
        out_shape=[jax.ShapeDtypeStruct(shape, bf16)] * 3,
        in_specs=[
            pl.BlockSpec(memory_space=pltpu.SMEM),
            pl.BlockSpec(memory_space=pltpu.VMEM),
        ]
        + [pl.BlockSpec(memory_space=pl.ANY)] * 4,
        out_specs=[pl.BlockSpec(memory_space=pltpu.VMEM)] * 3,
        scratch_shapes=[
            vmem((256, 1024), bf16),
            vmem((256, 1024), bf16),
            vmem((256, 1024), bf16),
            vmem((128, 1024), bf16),
            vmem((PLANE, 3 * HEAD, CHUNK), bf16),
            vmem((PLANE + 2, 3 * HEAD, CHUNK), bf16),
            vmem((PLANE, HEAD, BLOCK), bf16),
            vmem((4, HEAD, BLOCK), bf16),
            vmem((PLANE, 3, CHUNK, CHUNK), bf16),
            vmem((UNITS, MEM, HEAD, BLOCK), bf16),
            vmem((UNITS, MEM, HEAD, BLOCK), bf16),
            vmem((UNITS, MEM, HEAD, BLOCK), bf16),
            vmem((UNITS, MEM, HEAD, BLOCK), bf16),
            vmem((PLANE + 2, 2 * HEAD, CHUNK), jnp.float32),
            vmem((2 * HEAD, CHUNK), bf16),
            vmem((2 * HEAD, CHUNK), bf16),
            vmem((PLANE, HEAD, CHUNK), bf16),
            vmem((PLANE + 2, 2 * HEAD, CHUNK), bf16),
            vmem((PLANE, HEAD, CHUNK), bf16),
            vmem((PLANE, 2 * HEAD, CHUNK), bf16),
            dma((4,)),
            dma((16,)),
            dma((16,)),
            dma((16,)),
            dma((4,)),
            dma((2,)),
            dma((2,)),
            dma((UNITS, MEM)),
            dma((UNITS, MEM)),
            dma((UNITS, MEM)),
            dma((UNITS, MEM)),
            dma((2,)),
            dma((2,)),
            dma((PLANE,)),
            dma((PLANE,)),
            dma((PLANE,)),
            dma((PLANE,)),
        ],
        compiler_params=pltpu.CompilerParams(
            collective_id=0, has_side_effects=True, vmem_limit_bytes=48 << 20
        ),
        name="band_attention",
    )(widths, node_order.reshape(1, BLOCK), queries, keys, values, truth)


def solution(mesh):
    placed = (
        P("mem", "grid", None),
        P("mem", "grid", None),
        P("mem", "grid", None),
        P("grid", None),
        P(),
        P(),
    )
    return jax.shard_map(
        on_device,
        mesh=mesh,
        in_specs=placed,
        out_specs=(P("mem", "grid", None), P("mem", "grid", None), P("mem", "grid", None)),
        check_vma=False,
    )
```

time: 398 us -> 104 us (0.26)
  waiting for transfers between devices: 214 us -> 0 us
  Pallas kernels: 0 us -> 95.3 us
  local copies, waits for them, and re-layouts: 82.8 us -> 7.2 us
  starting transfers between devices: 43.4 us -> 0 us
  matrix products: 30.7 us -> 0 us
  other arithmetic: 24.7 us -> 0 us
    ppermute x4 -> x0, waiting for transfers between devices: 188 us -> none  [the longest x2 89 us: passed_along(): return lax.ppermute(block, axis, route)]
    pallas_call x0 -> x1, Pallas kernels: none -> 95.3 us  [on_device(): pl.pallas_call(kernel, out_shape=[jax.ShapeDtypeStruct(shape, bf16)] * 3,...]
    dynamic_slice x27 -> x0, local copies, waits for them, and re-layouts: 36.3 us -> none  [the longest x14 14.2 us: rows_at(): return split_heads(lax.dynamic_slice_in_dim(array, start, count, 0))]
    ppermute x4 -> x0, starting transfers between devices: 33.3 us -> none  [the longest x1 17.9 us: with_halo(): lax.ppermute(lax.slice_in_dim(block, 0, width, axis=dim), axis, backward)]
    dot_general x14 -> x0, matrix products: 30.7 us -> none  [the longest x4 8.99 us: masked_scores(): jnp.einsum('qhd,khd->hqk', query_part, key_part, preferred_element_type=j...]
    all_to_all x2 -> x0, waiting for transfers between devices: 25.7 us -> none  [the longest x1 14.4 us: on_device(): lax.all_to_all(member_grads, 'mem', split_axis=0, concat_axis=1, tiled=True)]
    dynamic_update_slice x12 -> x0, local copies, waits for them, and re-layouts: 21.1 us -> none  [the longest x4 13.8 us: back_step(): value_acc = lax.dynamic_update_slice_in_dim(value_acc, value_now, start, 0)]
    all_to_all x2 -> x0, starting transfers between devices: 10.1 us -> none  [the longest x1 5.22 us: on_device(): lax.all_to_all(outputs[None], 'mem', split_axis=1, concat_axis=0, tiled=T...]
  transfers between devices with their start and end apart: 6 -> 0, of which waited for: 5 -> 0; matrix products, arithmetic and copies ran while one was open for 1% -> 0% of each run, Pallas kernels for 0% -> 0%
where the time goes in v1:
time: 104 us; the launch traced here: 103 us
  Pallas kernels  95.3 us (92%)
  local copies, waits for them, and re-layouts  7.2 us (7%)
    pallas_call x1, Pallas kernels, on_device(): pl.pallas_call(kernel, out_shape=[jax.ShapeDtypeStruct(shape, bf16)] * 3,...  95.3 us
    unnamed x15, local copies, waits for them, and re-layouts  7.2 us

profile of v1, /device:TPU:1, one launch (start us, length us, event | category | flops | bytes accessed | tf_op | source)
XLA Modules:
  0.0 103.2 jit_solution(1439279750724426830)
XLA Ops:
  0.6 0.0 copy-start.5
  0.6 0.0 copy-start.4
  0.7 0.6 copy-done.5
  1.3 0.0 copy-done.4
  1.3 0.0 copy-start
  1.3 1.0 %copy-done = bf16[1,256,1024]{2,1,0:T(8,128)(2,1)S(1)} copy-done((bf16[1,256,1024]{2,1,0:T(8,128)(2,1)S(1)}, bf16[1,256,1024]{2,1,0:T(8,128)(2,1)}, u32[]{:S(2)}) %copy-start) | copy-done | bytes 524312
  2.3 0.0 copy-start.1
  2.3 1.0 %copy-done.1 = bf16[1,256,1024]{2,1,0:T(8,128)(2,1)S(1)} copy-done((bf16[1,256,1024]{2,1,0:T(8,128)(2,1)S(1)}, bf16[1,256,1024]{2,1,0:T(8,128)(2,1)}, u32[]{:S(2)}) %copy-start.1) | copy-done | bytes 524312
  3.4 0.0 copy-start.2
  3.4 1.0 %copy-done.2 = bf16[1,256,1024]{2,1,0:T(8,128)(2,1)S(1)} copy-done((bf16[1,256,1024]{2,1,0:T(8,128)(2,1)S(1)}, bf16[1,256,1024]{2,1,0:T(8,128)(2,1)}, u32[]{:S(2)}) %copy-start.2) | copy-done | bytes 524312
  4.4 0.0 copy-start.3
  4.4 1.0 %copy-done.3 = bf16[256,1024]{1,0:T(8,128)(2,1)S(1)} copy-done((bf16[256,1024]{1,0:T(8,128)(2,1)S(1)}, bf16[256,1024]{1,0:T(8,128)(2,1)}, u32[]{:S(2)}) %copy-start.3) | copy-done | bytes 524312
  5.5 95.3 %band_attention.1 = (bf16[1,256,1024]{2,1,0:T(8,128)(2,1)S(1)}, bf16[1,256,1024]{2,1,0:T(8,128)(2,1)S(1)}, bf16[1,256,1024]{2,1,0:T(8,128)(2,1)S(1)}) custom-call(s32[16]{0:T(128)S(1)} %copy-done.4, s32[1,128]{1,0:T(1,128)S(1)} %bitcast.1, bf16[1,256,1024]{2,1,0:T(8,128)(2,1)S(1)} %copy-done, bf16[1,256,1024]{2,1,0:T(8,128)(2,1)S(1)} %copy-done.1, ...), custom_call_target="tpu_custom_call" | custom-call | tf_op jit(solution)/shard_map/band_attention/pallas_call | solution.py:444
  100.8 0.8 copy.12
  101.6 0.8 copy.13
  102.4 0.8 copy.14
Async XLA Ops:
  0.6 0.7 copy-start.5
  0.6 0.7 copy-start.4
  1.3 1.0 %copy-start = (bf16[1,256,1024]{2,1,0:T(8,128)(2,1)S(1)}, bf16[1,256,1024]{2,1,0:T(8,128)(2,1)}, u32[]{:S(2)}) copy-start(bf16[1,256,1024]{2,1,0:T(8,128)(2,1)} %q_hbm.1) | copy-start | bytes 1572868
  2.3 1.0 %copy-start.1 = (bf16[1,256,1024]{2,1,0:T(8,128)(2,1)S(1)}, bf16[1,256,1024]{2,1,0:T(8,128)(2,1)}, u32[]{:S(2)}) copy-start(bf16[1,256,1024]{2,1,0:T(8,128)(2,1)} %k_hbm.1) | copy-start | bytes 1572868
  3.4 1.0 %copy-start.2 = (bf16[1,256,1024]{2,1,0:T(8,128)(2,1)S(1)}, bf16[1,256,1024]{2,1,0:T(8,128)(2,1)}, u32[]{:S(2)}) copy-start(bf16[1,256,1024]{2,1,0:T(8,128)(2,1)} %v_hbm.1) | copy-start | bytes 1572868
  4.4 1.0 %copy-start.3 = (bf16[256,1024]{1,0:T(8,128)(2,1)S(1)}, bf16[256,1024]{1,0:T(8,128)(2,1)}, u32[]{:S(2)}) copy-start(bf16[256,1024]{1,0:T(8,128)(2,1)} %t_hbm.1) | copy-start | bytes 1572868

commit v2 on v1

v2 whole, which is shorter than its diff:
```python
import functools

import jax
import jax.numpy as jnp
from jax import lax
from jax.experimental import pallas as pl
from jax.experimental.pallas import tpu as pltpu
from jax.sharding import PartitionSpec as P

HEAD = 64
BLOCK = 128
CHUNK = 2 * BLOCK
PLANE = 16
MEM = 8
UNITS = 4
NEG = -1e30
SMOOTH2 = 0.0625
SHARE = 16
MESH = pl.DeviceIdType.MESH

TN = (((0,), (0,)), ((), ()))
NT = (((1,), (1,)), ((), ()))
NN = (((1,), (0,)), ((), ()))


def dot(a, b, dims):
    return lax.dot_general(a, b, dims, preferred_element_type=jnp.float32)


def slope(diff):
    return diff * lax.rsqrt(diff * diff + SMOOTH2)


def kernel(
    widths, order, q_hbm, k_hbm, v_hbm, t_hbm,
    dq_out, dk_out, dv_out,
    q_in, k_in, v_in, t_in,
    stage, ext, k_nat, v_nat, tstage, tgt, weights, share, out_u, ens, gout, g_u, acc, back_low, back_high,
    dq_src, dkv_src, dq_dst, dkv_dst,
    load_sem, in_send, in_recv, t_send, t_recv, halo_send, halo_recv,
    m1_send, m1_recv, m2_send, m2_recv, back_send, back_recv,
    dq_send, dq_recv, dkv_send, dkv_recv,
):
    grid = lax.axis_index("grid")
    mem = lax.axis_index("mem")
    z_hi = grid // 16
    x = (grid // 4) % 4
    y = grid % 4
    p = grid % 16
    z_lo = mem // 2
    core = mem % 2
    f32, bf16 = jnp.float32, jnp.bfloat16

    def at_plane(xx, yy):
        return (z_hi * 16 + (xx % 4) * 4 + yy % 4, mem)

    def at_z(d):
        return (((z_hi + d) % 4) * 16 + p, mem)

    own_rows = pl.ds(pl.multiple_of(z_lo * SHARE, SHARE), SHARE)
    loads = [
        pltpu.make_async_copy(src.at[0], dst, load_sem.at[i])
        for i, (src, dst) in enumerate(((q_hbm, q_in), (k_hbm, k_in), (v_hbm, v_in)))
    ]
    for load in loads:
        load.start()
    load_truth = pltpu.make_async_copy(
        t_hbm.at[pl.ds(pl.multiple_of(core * BLOCK, BLOCK), BLOCK)], t_in, load_sem.at[3]
    )
    load_truth.start()

    offsets = [(dx, dy) for dx in (0, 3, 2, 1) for dy in (1, 3, 2, 0)]
    offsets.remove((0, 0))
    barrier = pltpu.get_barrier_semaphore()
    for dx, dy in offsets:
        pl.semaphore_signal(barrier, inc=1, device_id=at_plane(x + dx, y + dy), device_id_type=MESH)
    for o in range(1, MEM):
        pl.semaphore_signal(barrier, inc=1, device_id=(grid, (mem + o) % MEM), device_id_type=MESH)
    for d in (1, 3):
        pl.semaphore_signal(barrier, inc=1, device_id=at_z(d), device_id_type=MESH)

    for load in loads:
        load.wait()

    def to_stage(pair, parts):
        lanes = pl.ds(pl.multiple_of(pair * 128, 128), 128)
        for i in parts:
            block = (q_in, k_in, v_in)[i][:, lanes]
            if i == 0:
                block = block * bf16(0.125)
            block = block.T
            stage[pair * 2, pl.ds(i * HEAD, HEAD)] = block[:HEAD]
            stage[pair * 2 + 1, pl.ds(i * HEAD, HEAD)] = block[HEAD:]

    part_rows = (pl.ds(0, 2 * HEAD), pl.ds(2 * HEAD, HEAD))

    def in_copy(dx, dy, part):
        target = ((x + dx) % 4) * 4 + (y + dy) % 4
        return pltpu.make_async_remote_copy(
            src_ref=stage.at[target, part_rows[part]],
            dst_ref=ext.at[1 + p, part_rows[part]],
            send_sem=in_send.at[part, dx * 4 + dy],
            recv_sem=in_recv.at[part, dx * 4 + dy],
            device_id=at_plane(x + dx, y + dy),
            device_id_type=MESH,
        )

    for dx in (0, 3, 2, 1):
        row = (x + dx) % 4
        to_stage(row * 2, (0, 1))
        to_stage(row * 2 + 1, (0, 1))
        if dx == 0:
            pl.semaphore_wait(barrier, 15 + 7 + 2)
        for a, b in offsets:
            if a == dx:
                in_copy(a, b, 0).start()

    for pair in range(8):
        to_stage(pair, (2,))
    ext[1 + p] = stage[p]

    load_truth.wait()

    def t_copy(dx, dy):
        return pltpu.make_async_remote_copy(
            src_ref=tstage.at[((x + dx) % 4) * 4 + (y + dy) % 4, own_rows],
            dst_ref=tgt.at[p],
            send_sem=t_send.at[dx * 4 + dy],
            recv_sem=t_recv.at[p],
            device_id=at_plane(x + dx, y + dy),
            device_id_type=MESH,
        )

    nodes = lax.broadcasted_iota(jnp.int32, (BLOCK, BLOCK), 0)
    pick = jnp.where(nodes == order[...], 1.0, 0.0).astype(bf16)
    for pair in range(8):
        ordered = dot(t_in[:, pair * 128 : pair * 128 + 128], pick, TN).astype(bf16)
        tstage[pair * 2] = ordered[:HEAD]
        tstage[pair * 2 + 1] = ordered[HEAD:]
    tgt[p] = tstage[p, own_rows]

    acc[...] = jnp.zeros_like(acc)
    for corner in ((pl.ds(0, BLOCK), pl.ds(BLOCK, BLOCK)), (pl.ds(5 * BLOCK, BLOCK), pl.ds(0, BLOCK))):
        for j in range(PLANE):
            weights[j, corner[0], corner[1]] = jnp.zeros((BLOCK, BLOCK), bf16)

    for dx, dy in offsets:
        in_copy(dx, dy, 0).wait_send()
    for dx, dy in offsets:
        in_copy(dx, dy, 1).start()
    for dx, dy in offsets:
        t_copy(dx, dy).start()

    far = jnp.where(widths[p] >= 2, 0.0, NEG).astype(f32)

    def halo_copy(up, part):
        src, dst = (PLANE, 0) if up else (1, PLANE + 1)
        i = (0 if up else 1) + 2 * part
        rows = pl.ds((1 + part) * HEAD, HEAD)
        return pltpu.make_async_remote_copy(
            src_ref=ext.at[src, rows],
            dst_ref=ext.at[dst, rows],
            send_sem=halo_send.at[i],
            recv_sem=halo_recv.at[i],
            device_id=at_z(1 if up else 3),
            device_id_type=MESH,
        )

    def natural(slot, part):
        (k_nat, v_nat)[part][slot] = ext[slot, pl.ds((1 + part) * HEAD, HEAD)].T

    def all_natural(part):
        def one(slot, carry):
            natural(slot, part)
            return carry

        lax.fori_loop(1, PLANE + 1, one, 0)

    def arrive(part):
        for dx, dy in offsets:
            in_copy(dx, dy, part).wait_recv()
        for up in (True, False):
            halo_copy(up, part).start()

    def arrive_halos(part):
        for up in (True, False):
            halo_copy(up, part).wait_recv()
        natural(0, part)
        natural(PLANE + 1, part)

    def unit_of(k):
        unit = (x + 1 + k) % 4
        return jnp.where(x == 2, 3 * k, unit) if k < 2 else unit

    def m1_copy(k, o):
        to = (mem + o) % MEM
        return pltpu.make_async_remote_copy(
            src_ref=out_u.at[k, to % 2, pl.ds(pl.multiple_of(to // 2 * SHARE, SHARE), SHARE)],
            dst_ref=ens.at[k, mem],
            send_sem=m1_send.at[k, o],
            recv_sem=m1_recv.at[k, o],
            device_id=(grid, (mem + o) % MEM),
            device_id_type=MESH,
        )

    def m2_copy(k, o):
        return pltpu.make_async_remote_copy(
            src_ref=gout.at[k, (mem + o) % MEM],
            dst_ref=g_u.at[k, core, own_rows],
            send_sem=m2_send.at[k, o],
            recv_sem=m2_recv.at[k, o],
            device_id=(grid, (mem + o) % MEM),
            device_id_type=MESH,
        )

    def lanes_of(i):
        return pl.ds(pl.multiple_of(i * BLOCK, BLOCK), BLOCK)

    def chunk_of(k, i):
        return (unit_of(k) * 4 + 1 + i) % PLANE

    def score(unit):
        def one(i, carry):
            j = (unit * 4 + 1 + i) % PLANE
            q_t = ext[j + 1, pl.ds(0, HEAD)]
            scores = [dot(k_nat[j + t], q_t, NN) for t in range(3)]
            for h in range(2):
                lanes = slice(h * BLOCK, h * BLOCK + BLOCK)
                tiles = []
                for n in range(5):
                    top = (h + n) % 2 * BLOCK
                    tiles.append(scores[(h + n) // 2][top : top + BLOCK, lanes])
                tiles[0] = tiles[0] + far
                tiles[4] = tiles[4] + far
                highest = functools.reduce(jnp.maximum, tiles)
                highest = jnp.max(highest, axis=0, keepdims=True)
                total = jnp.zeros((BLOCK, BLOCK), f32)
                for n in range(5):
                    term = jnp.exp(tiles[n] - highest)
                    total = total + term
                    weights[j, pl.ds((h + n) * BLOCK, BLOCK), lanes] = term.astype(bf16)
                share[j, :, lanes] = 1.0 / jnp.sum(total, axis=0, keepdims=True)
            return carry

        lax.fori_loop(0, 4, one, 0)

    def mix(k):
        if k == 1:
            arrive_halos(1)
        def one(i, carry):
            j = chunk_of(k, i)
            mixed = jnp.zeros((HEAD, CHUNK), f32)
            for t in range(3):
                mixed = mixed + dot(
                    ext[j + t, pl.ds(2 * HEAD, HEAD)], weights[j, pl.ds(t * CHUNK, CHUNK)], NN
                )
            mixed = (mixed * share[j]).astype(bf16)
            out_u[k, 0, :, lanes_of(i)] = mixed[:, :BLOCK]
            out_u[k, 1, :, lanes_of(i)] = mixed[:, BLOCK:]
            return carry

        lax.fori_loop(0, 4, one, 0)
        ens[k, mem] = out_u[k, core, own_rows]

    def m1_start(k):
        if k > 0:
            for o in range(1, MEM):
                m1_copy(k - 1, o).wait_send()
        for o in (1, 7, 2, 6, 3, 5, 4):
            m1_copy(k, o).start()

    def truth_arrive(k):
        for i in range(4):
            j = chunk_of(k, i)

            @pl.when(j != p)
            def _():
                pltpu.make_async_remote_copy(
                    src_ref=tstage.at[0, own_rows],
                    dst_ref=tgt.at[j],
                    send_sem=t_send.at[0],
                    recv_sem=t_recv.at[j],
                    device_id=(z_hi * 16 + j, mem),
                    device_id_type=MESH,
                ).wait_recv()

    def crps(k):
        truth_arrive(k)
        for o in range(1, MEM):
            m1_copy(k, o).wait_recv()
        own = [ens[k, n].astype(f32) for n in range(MEM)]
        target = jnp.concatenate([tgt[chunk_of(k, i)] for i in range(4)], axis=1).astype(f32)
        totals = [jnp.zeros((SHARE, UNITS * BLOCK), f32) for _ in range(MEM)]
        for a in range(MEM):
            for b in range(a + 1, MEM):
                s = slope(own[a] - own[b])
                totals[a] = totals[a] + s
                totals[b] = totals[b] - s
        for n in range(MEM):
            gout[k, n] = (slope(own[n] - target) - totals[n] * (1.0 / (MEM - 1))).astype(bf16)
        for o in (1, 7, 2, 6, 3, 5, 4):
            m2_copy(k, o).start()
        g_u[k, core, own_rows] = gout[k, mem]

    def dq_copy(j):
        return pltpu.make_async_remote_copy(
            src_ref=dq_src.at[j],
            dst_ref=dq_dst.at[p],
            send_sem=dq_send.at[j],
            recv_sem=dq_recv.at[p],
            device_id=(z_hi * 16 + j, mem),
            device_id_type=MESH,
        )

    def dkv_copy(j):
        return pltpu.make_async_remote_copy(
            src_ref=dkv_src.at[j],
            dst_ref=dkv_dst.at[p],
            send_sem=dkv_send.at[j],
            recv_sem=dkv_recv.at[p],
            device_id=(z_hi * 16 + j, mem),
            device_id_type=MESH,
        )

    def back_copy(down):
        i = 0 if down else 1
        return pltpu.make_async_remote_copy(
            src_ref=dkv_src.at[PLANE + i],
            dst_ref=(back_high if down else back_low),
            send_sem=back_send.at[i],
            recv_sem=back_recv.at[i],
            device_id=at_z(3 if down else 1),
            device_id_type=MESH,
        )

    def finish_dkv(j):
        dkv_src[j] = acc[j + 1].astype(bf16)

        @pl.when(j != p)
        def _():
            dkv_copy(j).start()

        @pl.when(j == p)
        def _():
            dkv_dst[p] = dkv_src[p]

    def finish_ends():
        back_copy(True).wait_recv()
        acc[PLANE] += back_high[...].astype(f32)
        finish_dkv(PLANE - 1)
        back_copy(False).wait_recv()
        acc[1] += back_low[...].astype(f32)
        finish_dkv(0)

    left = lax.broadcasted_iota(jnp.int32, (CHUNK, 2 * HEAD), 1) < HEAD

    def backward(k):
        for o in range(1, MEM):
            m2_copy(k, o).wait_recv()

        def one(i):
            j = chunk_of(k, i)
            g_t = jnp.concatenate([g_u[k, c, :, lanes_of(i)] for c in range(2)], axis=1).astype(f32)
            o_t = jnp.concatenate([out_u[k, c, :, lanes_of(i)] for c in range(2)], axis=1).astype(f32)
            scale = share[j]
            inner = jnp.sum(g_t * o_t, axis=0, keepdims=True) * scale
            g_t = (g_t * scale).astype(bf16)
            both = jnp.concatenate([ext[j + 1, pl.ds(0, HEAD)], g_t], axis=0).T
            q_side = jnp.where(left, both, bf16(0))
            g_side = jnp.where(left, bf16(0), both)
            dq = jnp.zeros((HEAD, CHUNK), f32)
            for t in range(3):
                along = dot(v_nat[j + t], g_t, NN)
                low = weights[j, pl.ds(t * CHUNK, CHUNK)]
                ds = (low.astype(f32) * (along - inner)).astype(bf16)
                dq = dq + dot(ext[j + t, pl.ds(HEAD, HEAD)], ds, NN)
                acc[j + t] += dot(ds, q_side, NN) + dot(low, g_side, NN)
            dq_src[j] = (dq * 0.125).astype(bf16)

            @pl.when(j != p)
            def _():
                dq_copy(j).start()

            @pl.when(j == p)
            def _():
                dq_dst[p] = dq_src[p]

        def ends(n, carry):
            one(3 - n)
            return carry

        lax.fori_loop(0, 2, ends, 0)

        @pl.when(unit_of(k) == 3)
        def _():
            dkv_src[PLANE] = acc[0].astype(bf16)
            back_copy(True).start()
            dkv_src[PLANE + 1] = acc[PLANE + 1].astype(bf16)
            back_copy(False).start()

        def others(i, carry):
            one(i)
            return carry

        lax.fori_loop(0, 2, others, 0)

        def done(i, carry):
            j = (unit_of(k) * 4 + i) % PLANE

            @pl.when((j != 0) & (j != PLANE - 1))
            def _():
                finish_dkv(j)

            return carry

        if k == 1:

            @pl.when(x == 2)
            def _():
                finish_dkv(PLANE - 2)
                finish_dkv(1)

            @pl.when(x != 2)
            def _():
                lax.fori_loop(0, 4, done, 0)
        else:
            lax.fori_loop(2 if k == 0 else 0, 6 if k == UNITS - 1 else 4, done, 0)
        if k == 2:
            pl.when((x == 1) | (x == 2))(finish_ends)
        if k == 3:
            pl.when((x == 0) | (x == 3))(finish_ends)

    arrive(0)
    all_natural(0)
    for unit in range(3):
        score(unit)
    arrive(1)
    mix(0)
    m1_start(0)
    arrive_halos(0)
    score(3)
    mix(1)
    mix(2)
    mix(3)
    m1_start(1)
    all_natural(1)
    crps(0)
    m1_start(2)
    crps(1)
    m1_start(3)
    backward(0)
    crps(2)
    backward(1)
    crps(3)
    backward(2)
    backward(3)

    def all_arrived(ref, recv):
        def one(n, carry):
            src = (p + n) % PLANE
            pltpu.make_async_remote_copy(
                src_ref=ref.at[src], dst_ref=ref.at[src], send_sem=dq_send.at[0], recv_sem=recv.at[src],
                device_id=(z_hi * 16 + src, mem), device_id_type=MESH,
            ).wait_recv()
            return carry

        lax.fori_loop(1, PLANE, one, 0)

    all_arrived(dq_dst, dq_recv)
    for pair in range(8):
        block = jnp.concatenate([dq_dst[2 * pair], dq_dst[2 * pair + 1]], axis=0)
        dq_out[0, :, pair * 128 : pair * 128 + 128] = block.T
    all_arrived(dkv_dst, dkv_recv)
    for pair in range(8):
        even, odd = dkv_dst[2 * pair], dkv_dst[2 * pair + 1]
        lanes = slice(pair * 128, pair * 128 + 128)
        dk_out[0, :, lanes] = jnp.concatenate([even[:, :HEAD], odd[:, :HEAD]], axis=1)
        dv_out[0, :, lanes] = jnp.concatenate([even[:, HEAD:], odd[:, HEAD:]], axis=1)

    for dx, dy in offsets:
        in_copy(dx, dy, 1).wait_send()
    for up in (True, False):
        for part in range(2):
            halo_copy(up, part).wait_send()
        back_copy(up).wait_send()
    for o in range(1, MEM):
        m1_copy(UNITS - 1, o).wait_send()
        for k in range(UNITS):
            m2_copy(k, o).wait_send()

    for dx, dy in offsets:
        t_copy(dx, dy).wait_send()

    def sent(n, carry):
        j = (p + n) % PLANE
        dq_copy(j).wait_send()
        dkv_copy(j).wait_send()
        return carry

    lax.fori_loop(1, PLANE, sent, 0)


def on_device(queries, keys, values, truth, widths, node_order):
    bf16 = jnp.bfloat16
    shape = queries.shape
    dma = pltpu.SemaphoreType.DMA
    vmem = pltpu.VMEM
    return pl.pallas_call(
        kernel,
        out_shape=[jax.ShapeDtypeStruct(shape, bf16)] * 3,
        in_specs=[
            pl.BlockSpec(memory_space=pltpu.SMEM),
            pl.BlockSpec(memory_space=pltpu.VMEM),
        ]
        + [pl.BlockSpec(memory_space=pl.ANY)] * 4,
        out_specs=[pl.BlockSpec(memory_space=pltpu.VMEM)] * 3,
        scratch_shapes=[
            vmem((256, 1024), bf16),
            vmem((256, 1024), bf16),
            vmem((256, 1024), bf16),
            vmem((128, 1024), bf16),
            vmem((PLANE, 3 * HEAD, CHUNK), bf16),
            vmem((PLANE + 2, 3 * HEAD, CHUNK), bf16),
            vmem((PLANE + 2, CHUNK, HEAD), bf16),
            vmem((PLANE + 2, CHUNK, HEAD), bf16),
            vmem((PLANE, HEAD, BLOCK), bf16),
            vmem((PLANE, SHARE, BLOCK), bf16),
            vmem((PLANE, 3 * CHUNK, CHUNK), bf16),
            vmem((PLANE, 1, CHUNK), jnp.float32),
            vmem((UNITS, 2, HEAD, 4 * BLOCK), bf16),
            vmem((UNITS, MEM, SHARE, 4 * BLOCK), bf16),
            vmem((UNITS, MEM, SHARE, 4 * BLOCK), bf16),
            vmem((UNITS, 2, HEAD, 4 * BLOCK), bf16),
            vmem((PLANE + 2, CHUNK, 2 * HEAD), jnp.float32),
            vmem((CHUNK, 2 * HEAD), bf16),
            vmem((CHUNK, 2 * HEAD), bf16),
            vmem((PLANE, HEAD, CHUNK), bf16),
            vmem((PLANE + 2, CHUNK, 2 * HEAD), bf16),
            vmem((PLANE, HEAD, CHUNK), bf16),
            vmem((PLANE, CHUNK, 2 * HEAD), bf16),
            dma((4,)),
            dma((2, 16)),
            dma((2, 16)),
            dma((16,)),
            dma((16,)),
            dma((4,)),
            dma((4,)),
            dma((UNITS, MEM)),
            dma((UNITS, MEM)),
            dma((UNITS, MEM)),
            dma((UNITS, MEM)),
            dma((2,)),
            dma((2,)),
            dma((PLANE,)),
            dma((PLANE,)),
            dma((PLANE,)),
            dma((PLANE,)),
        ],
        compiler_params=pltpu.CompilerParams(
            collective_id=0, has_side_effects=True, vmem_limit_bytes=62 << 20
        ),
        name="band_attention",
    )(widths, node_order.reshape(1, BLOCK), queries, keys, values, truth)


def solution(mesh):
    placed = (
        P("mem", "grid", None),
        P("mem", "grid", None),
        P("mem", "grid", None),
        P("grid", None),
        P(),
        P(),
    )
    return jax.shard_map(
        on_device,
        mesh=mesh,
        in_specs=placed,
        out_specs=(P("mem", "grid", None), P("mem", "grid", None), P("mem", "grid", None)),
        check_vma=False,
    )
```

time: 104 us -> 92.1 us (0.89)
  Pallas kernels: 95.3 us -> 86.6 us
  local copies, waits for them, and re-layouts: 7.2 us -> 3.95 us
    pallas_call x1, Pallas kernels: 95.3 us -> 86.6 us  [on_device(): pl.pallas_call(kernel, out_shape=[jax.ShapeDtypeStruct(shape, bf16)] * 3,...]
    unnamed x15 -> x7, local copies, waits for them, and re-layouts: 7.2 us -> 3.95 us
where the time goes in v2:
time: 92.1 us; the launch traced here: 91.2 us
  Pallas kernels  86.6 us (94%)
  local copies, waits for them, and re-layouts  3.95 us (4%)
    pallas_call x1, Pallas kernels, on_device(): pl.pallas_call(kernel, out_shape=[jax.ShapeDtypeStruct(shape, bf16)] * 3,...  86.6 us
    unnamed x7, local copies, waits for them, and re-layouts  3.95 us

profile of v2, /device:TPU:1, one launch (start us, length us, event | category | flops | bytes accessed | tf_op | source)
XLA Modules:
  0.0 91.2 jit_solution(8876084049656094022)
XLA Ops:
  0.6 86.6 %band_attention.1 = (bf16[1,256,1024]{2,1,0:T(8,128)(2,1)}, bf16[1,256,1024]{2,1,0:T(8,128)(2,1)}, bf16[1,256,1024]{2,1,0:T(8,128)(2,1)}) custom-call(s32[16]{0:T(128)} %widths.1, s32[1,128]{1,0:T(1,128)} %bitcast.1, bf16[1,256,1024]{2,1,0:T(8,128)(2,1)} %q_hbm.1, bf16[1,256,1024]{2,1,0:T(8,128)(2,1)} %k_hbm.1, bf16[1,256,1024]{2,1,0:T(8,128)(2,1)} %v_hbm.1, ...), custom_call_target="tpu_custom_call" | custom-call | tf_op jit(solution)/shard_map/band_attention/pallas_call | solution.py:508
  87.2 0.0 copy-start.1
  87.2 1.9 %copy.12 = bf16[1,256,1024]{2,1,0:T(8,128)(2,1)} copy(bf16[1,256,1024]{2,1,0:T(8,128)(2,1)} %get-tuple-element.6) | data formatting | bytes 1048576
  89.2 0.0 copy-done.1
  89.2 0.0 copy-start
  89.2 0.8 copy.13
  90.0 0.4 copy-done
  90.4 0.8 copy.14
Async XLA Ops:
  87.2 1.9 %copy-start.1 = (bf16[1,256,1024]{2,1,0:T(8,128)(2,1)S(1)}, bf16[1,256,1024]{2,1,0:T(8,128)(2,1)}, u32[]{:S(2)}) copy-start(bf16[1,256,1024]{2,1,0:T(8,128)(2,1)} %get-tuple-element.7) | copy-start | bytes 1572868
  89.2 1.2 %copy-start = (bf16[1,256,1024]{2,1,0:T(8,128)(2,1)S(1)}, bf16[1,256,1024]{2,1,0:T(8,128)(2,1)}, u32[]{:S(2)}) copy-start(bf16[1,256,1024]{2,1,0:T(8,128)(2,1)} %get-tuple-element.8) | copy-start | bytes 1572868

commit v3 on v2

--- a/solution.py
+++ b/solution.py
@@ -33,10 +33,10 @@
 
 def kernel(
     widths, order, q_hbm, k_hbm, v_hbm, t_hbm,
-    dq_out, dk_out, dv_out,
+    dq_dst, dkv_dst,
     q_in, k_in, v_in, t_in,
     stage, ext, k_nat, v_nat, tstage, tgt, weights, share, out_u, ens, gout, g_u, acc, back_low, back_high,
-    dq_src, dkv_src, dq_dst, dkv_dst,
+    dq_src, dkv_src,
     load_sem, in_send, in_recv, t_send, t_recv, halo_send, halo_recv,
     m1_send, m1_recv, m2_send, m2_recv, back_send, back_recv,
     dq_send, dq_recv, dkv_send, dkv_recv,
@@ -92,7 +92,11 @@
             stage[pair * 2, pl.ds(i * HEAD, HEAD)] = block[:HEAD]
             stage[pair * 2 + 1, pl.ds(i * HEAD, HEAD)] = block[HEAD:]
 
-    part_rows = (pl.ds(0, 2 * HEAD), pl.ds(2 * HEAD, HEAD))
+    is_end = (p == 0) | (p == PLANE - 1)
+    part_rows = (
+        pl.ds(pl.multiple_of(jnp.where(is_end, HEAD, 0), HEAD), 2 * HEAD),
+        pl.ds(pl.multiple_of(jnp.where(is_end, 0, 2 * HEAD), HEAD), HEAD),
+    )
 
     def in_copy(dx, dy, part):
         target = ((x + dx) % 4) * 4 + (y + dy) % 4
@@ -107,16 +111,14 @@
 
     for dx in (0, 3, 2, 1):
         row = (x + dx) % 4
-        to_stage(row * 2, (0, 1))
-        to_stage(row * 2 + 1, (0, 1))
+        to_stage(row * 2, (0, 1, 2))
+        to_stage(row * 2 + 1, (0, 1, 2))
         if dx == 0:
             pl.semaphore_wait(barrier, 15 + 7 + 2)
         for a, b in offsets:
             if a == dx:
                 in_copy(a, b, 0).start()
 
-    for pair in range(8):
-        to_stage(pair, (2,))
     ext[1 + p] = stage[p]
 
     load_truth.wait()
@@ -179,8 +181,10 @@
     def arrive(part):
         for dx, dy in offsets:
             in_copy(dx, dy, part).wait_recv()
-        for up in (True, False):
-            halo_copy(up, part).start()
+        if part == 0:
+            for up in (True, False):
+                halo_copy(up, 0).start()
+                halo_copy(up, 1).start()
 
     def arrive_halos(part):
         for up in (True, False):
@@ -467,16 +471,7 @@
         lax.fori_loop(1, PLANE, one, 0)
 
     all_arrived(dq_dst, dq_recv)
-    for pair in range(8):
-        block = jnp.concatenate([dq_dst[2 * pair], dq_dst[2 * pair + 1]], axis=0)
-        dq_out[0, :, pair * 128 : pair * 128 + 128] = block.T
     all_arrived(dkv_dst, dkv_recv)
-    for pair in range(8):
-        even, odd = dkv_dst[2 * pair], dkv_dst[2 * pair + 1]
-        lanes = slice(pair * 128, pair * 128 + 128)
-        dk_out[0, :, lanes] = jnp.concatenate([even[:, :HEAD], odd[:, :HEAD]], axis=1)
-        dv_out[0, :, lanes] = jnp.concatenate([even[:, HEAD:], odd[:, HEAD:]], axis=1)
-
     for dx, dy in offsets:
         in_copy(dx, dy, 1).wait_send()
     for up in (True, False):
@@ -500,20 +495,32 @@
     lax.fori_loop(1, PLANE, sent, 0)
 
 
+def assemble(dq, dkv, dq_out, dk_out, dv_out):
+    for pair in range(dq.shape[0] // 2):
+        lanes = slice(pair * 128, pair * 128 + 128)
+        dq_out[0, :, lanes] = jnp.concatenate([dq[2 * pair], dq[2 * pair + 1]], axis=0).T
+        even, odd = dkv[2 * pair], dkv[2 * pair + 1]
+        dk_out[0, :, lanes] = jnp.concatenate([even[:, :HEAD], odd[:, :HEAD]], axis=1)
+        dv_out[0, :, lanes] = jnp.concatenate([even[:, HEAD:], odd[:, HEAD:]], axis=1)
+
+
 def on_device(queries, keys, values, truth, widths, node_order):
     bf16 = jnp.bfloat16
     shape = queries.shape
     dma = pltpu.SemaphoreType.DMA
     vmem = pltpu.VMEM
-    return pl.pallas_call(
+    dq, dkv = pl.pallas_call(
         kernel,
-        out_shape=[jax.ShapeDtypeStruct(shape, bf16)] * 3,
+        out_shape=[
+            jax.ShapeDtypeStruct((PLANE, HEAD, CHUNK), bf16),
+            jax.ShapeDtypeStruct((PLANE, CHUNK, 2 * HEAD), bf16),
+        ],
         in_specs=[
             pl.BlockSpec(memory_space=pltpu.SMEM),
             pl.BlockSpec(memory_space=pltpu.VMEM),
         ]
         + [pl.BlockSpec(memory_space=pl.ANY)] * 4,
-        out_specs=[pl.BlockSpec(memory_space=pltpu.VMEM)] * 3,
+        out_specs=[pl.BlockSpec(memory_space=pltpu.VMEM)] * 2,
         scratch_shapes=[
             vmem((256, 1024), bf16),
             vmem((256, 1024), bf16),
@@ -536,8 +543,6 @@
             vmem((CHUNK, 2 * HEAD), bf16),
             vmem((PLANE, HEAD, CHUNK), bf16),
             vmem((PLANE + 2, CHUNK, 2 * HEAD), bf16),
-            vmem((PLANE, HEAD, CHUNK), bf16),
-            vmem((PLANE, CHUNK, 2 * HEAD), bf16),
             dma((4,)),
             dma((2, 16)),
             dma((2, 16)),
@@ -561,6 +566,19 @@
         ),
         name="band_attention",
     )(widths, node_order.reshape(1, BLOCK), queries, keys, values, truth)
+    steps = 4
+    heads = PLANE // steps
+    return pl.pallas_call(
+        assemble,
+        grid=(steps,),
+        out_shape=[jax.ShapeDtypeStruct(shape, bf16)] * 3,
+        in_specs=[
+            pl.BlockSpec((heads, HEAD, CHUNK), lambda i: (i, 0, 0)),
+            pl.BlockSpec((heads, CHUNK, 2 * HEAD), lambda i: (i, 0, 0)),
+        ],
+        out_specs=[pl.BlockSpec((1, CHUNK, heads * HEAD), lambda i: (0, 0, i))] * 3,
+        name="assemble",
+    )(dq, dkv)
 
 
 def solution(mesh):

time: 92.1 us -> 89.7 us (0.974)
  local copies, waits for them, and re-layouts: 3.95 us -> 0 us
  Pallas kernels: 86.6 us -> 88.4 us
    unnamed x7 -> x0, local copies, waits for them, and re-layouts: 3.95 us -> none
    pallas_call x1 -> x2, Pallas kernels: 86.6 us -> 88.4 us  [the longest x1 84.6 us: on_device(): pl.pallas_call(kernel, out_shape=[jax.ShapeDtypeStruct((PLANE, HEAD, CHUN...]
where the time goes in v3:
time: 89.7 us; the launch traced here: 89 us
  Pallas kernels  88.4 us (99%)
    pallas_call x1, Pallas kernels, on_device(): pl.pallas_call(kernel, out_shape=[jax.ShapeDtypeStruct((PLANE, HEAD, CHUN...  84.6 us
    pallas_call x1, Pallas kernels, on_device(): pl.pallas_call(assemble, grid=(steps,), out_shape=[jax.ShapeDtypeStruct(s...  3.79 us

profile of v3, /device:TPU:1, one launch (start us, length us, event | category | flops | bytes accessed | tf_op | source)
XLA Modules:
  0.0 89.0 jit_solution(693770183765081917)
XLA Ops:
  0.6 84.6 %band_attention.1 = (bf16[16,64,256]{2,1,0:T(8,128)(2,1)}, bf16[16,256,128]{2,1,0:T(8,128)(2,1)}) custom-call(s32[16]{0:T(128)} %widths.1, s32[1,128]{1,0:T(1,128)} %bitcast.1, bf16[1,256,1024]{2,1,0:T(8,128)(2,1)} %q_hbm.1, bf16[1,256,1024]{2,1,0:T(8,128)(2,1)} %k_hbm.1, bf16[1,256,1024]{2,1,0:T(8,128)(2,1)} %v_hbm.1, bf16[256,1024]{1,0:T(8,128)(2,1)} %t_hbm.1), custom_call_target="tpu_custom_call" | custom-call | tf_op jit(solution)/shard_map/band_attention/pallas_call | solution.py:512
  85.2 3.8 %assemble.1 = (bf16[1,256,1024]{2,1,0:T(8,128)(2,1)}, bf16[1,256,1024]{2,1,0:T(8,128)(2,1)}, bf16[1,256,1024]{2,1,0:T(8,128)(2,1)}) custom-call(bf16[16,64,256]{2,1,0:T(8,128)(2,1)} %get-tuple-element.5.dq, bf16[16,256,128]{2,1,0:T(8,128)(2,1)} %get-tuple-element.6.dkv), custom_call_target="tpu_custom_call" | custom-call | tf_op jit(solution)/shard_map/assemble/pallas_call | solution.py:571

commit v4 on v3

--- a/solution.py
+++ b/solution.py
@@ -194,7 +194,7 @@
 
     def unit_of(k):
         unit = (x + 1 + k) % 4
-        return jnp.where(x == 2, 3 * k, unit) if k < 2 else unit
+        return jnp.where(x == 2, 3 * k, unit) if k < 2 else jnp.where(x == 3, 5 - k, unit)
 
     def m1_copy(k, o):
         to = (mem + o) % MEM
@@ -417,14 +417,14 @@
 
             return carry
 
-        if k == 1:
-
-            @pl.when(x == 2)
+        if k in (1, 2):
+
+            @pl.when(x == k + 1)
             def _():
                 finish_dkv(PLANE - 2)
                 finish_dkv(1)
 
-            @pl.when(x != 2)
+            @pl.when(x != k + 1)
             def _():
                 lax.fori_loop(0, 4, done, 0)
         else:

time: 89.7 us -> 90.1 us (level)
  no operation moved by 1% of the time
where the time goes in v4:
time: 90.1 us; the launch traced here: 89.7 us
  Pallas kernels  89 us (99%)
    pallas_call x1, Pallas kernels, on_device(): pl.pallas_call(kernel, out_shape=[jax.ShapeDtypeStruct((PLANE, HEAD, CHUN...  85.2 us
    pallas_call x1, Pallas kernels, on_device(): pl.pallas_call(assemble, grid=(steps,), out_shape=[jax.ShapeDtypeStruct(s...  3.79 us

profile of v4, /device:TPU:1, one launch (start us, length us, event | category | flops | bytes accessed | tf_op | source)
XLA Modules:
  0.0 89.7 jit_solution(713067588019853845)
XLA Ops:
  0.6 85.2 %band_attention.1 = (bf16[16,64,256]{2,1,0:T(8,128)(2,1)}, bf16[16,256,128]{2,1,0:T(8,128)(2,1)}) custom-call(s32[16]{0:T(128)} %widths.1, s32[1,128]{1,0:T(1,128)} %bitcast.1, bf16[1,256,1024]{2,1,0:T(8,128)(2,1)} %q_hbm.1, bf16[1,256,1024]{2,1,0:T(8,128)(2,1)} %k_hbm.1, bf16[1,256,1024]{2,1,0:T(8,128)(2,1)} %v_hbm.1, bf16[256,1024]{1,0:T(8,128)(2,1)} %t_hbm.1), custom_call_target="tpu_custom_call" | custom-call | tf_op jit(solution)/shard_map/band_attention/pallas_call | solution.py:512
  85.9 3.8 %assemble.1 = (bf16[1,256,1024]{2,1,0:T(8,128)(2,1)}, bf16[1,256,1024]{2,1,0:T(8,128)(2,1)}, bf16[1,256,1024]{2,1,0:T(8,128)(2,1)}) custom-call(bf16[16,64,256]{2,1,0:T(8,128)(2,1)} %get-tuple-element.5.dq, bf16[16,256,128]{2,1,0:T(8,128)(2,1)} %get-tuple-element.6.dkv), custom_call_target="tpu_custom_call" | custom-call | tf_op jit(solution)/shard_map/assemble/pallas_call | solution.py:571
